TPU v7x, 512 devices: a whole 4x4x16 slice. The times are simulated.
512 devices in a mesh: blk: 128 (over x, z, core), gz: 4 (over y).
Axes of the slice: x: 4, y: 4, z: 16, core: 2. Of those that a mesh axis runs over, the one named last changes fastest.
Arguments:
- fixed: bfloat16 [128, 32, 32, 128], P('blk', 'gz'), may hold values from -6 to 6
- moving: bfloat16 [128, 32, 32, 128], P('blk', 'gz'), may hold values from -6 to 6
- block_place: int32 [128], P('blk'), may hold values from 0 to 127, each once
- tissue: int32 [128], P('blk'), may hold values 0 or 1
Outputs:
- velocity: float32 [3, 2, 32, 64], replicated
- cc_map: float32 [128, 32, 32, 128], P('blk', 'gz')
Inputs may be any that keep to these rules, and one draw needn't show every extreme that they name: `block_place`: each block position from 0 to 127 is named by exactly one block.
All inputs are finite; a program needn't handle non-finite values. No bound on the sum of `tissue` on one device may be relied on, other than what follows from the above.
Results may differ from a plain program's by a relative error of at most 0.0004.
Values may be sent and summed in bfloat16 or wider, within the bound.
A program may use at most 64 MiB of HBM per device.

v0:
```python
import math
import jax
import jax.numpy as jnp
from jax import lax
from jax.sharding import PartitionSpec as P

SCALE = 16
GY = 8
ITERS = 2
EXACT = lax.Precision.HIGHEST
EPSILON = 1e-05
STEP_LENGTH = 0.5
BOX_TAPS = [1.0 / 9.0] * 9
GAUSS_RAW = [math.exp(-((offset - 3) ** 2) / 4.5) for offset in range(7)]
GAUSS_TAPS = [value / sum(GAUSS_RAW) for value in GAUSS_RAW]


def with_halo(block, sides, width):
    for axis, dim in sides:
        count = lax.axis_size(axis)
        forward = [(i, i + 1) for i in range(count - 1)]
        backward = [(target, source) for source, target in forward]
        low = lax.ppermute(
            lax.slice_in_dim(block, block.shape[dim] - width, None, axis=dim), axis, forward
        )
        high = lax.ppermute(lax.slice_in_dim(block, 0, width, axis=dim), axis, backward)
        block = jnp.concatenate([low, block, high], axis=dim)
    return block


def tap_matrix(count, taps):
    radius = len(taps) // 2
    rows = jnp.arange(count)[:, None]
    cols = jnp.arange(count)[None, :]
    matrix = jnp.zeros((count, count), jnp.float32)
    for offset, weight in enumerate(taps):
        matrix = matrix + weight * (rows - cols == offset - radius).astype(jnp.float32)
    return matrix


def along_rows(field, matrix):
    return jnp.einsum("...xy,xu->...uy", field, matrix, precision=EXACT)


def along_cols(field, matrix):
    return jnp.einsum("...y,yv->...v", field, matrix, precision=EXACT)


def planes_filter(field, taps, count):
    total = jnp.zeros(field.shape[:-3] + (count,) + field.shape[-2:], jnp.float32)
    for offset, weight in enumerate(taps):
        total = total + weight * field[..., offset : offset + count, :, :]
    return total


def slope(field, axis):
    widths = [(0, 0)] * field.ndim
    widths[axis] = (1, 1)
    padded = jnp.pad(field, widths)
    length = field.shape[axis]
    upper = lax.slice_in_dim(padded, 2, length + 2, axis=axis)
    lower = lax.slice_in_dim(padded, 0, length, axis=axis)
    return 0.5 * (upper - lower)


def hat_rows(coords, count):
    where = jnp.clip((coords + 0.5) / SCALE - 0.5, 0.0, count - 1.0)
    marks = jnp.arange(count).astype(jnp.float32)
    return jnp.maximum(0.0, 1.0 - jnp.abs(where[..., None] - marks))


def statistics(means, fixed_c, warped_c):
    sii = means[2] - means[0] * means[0]
    sww = means[3] - means[1] * means[1]
    siw = means[4] - means[0] * means[1]
    denom = sii * sww + EPSILON
    similar = siw * siw / denom
    weight = (
        2.0 * siw / denom * (fixed_c - means[0] - siw / (sww + EPSILON) * (warped_c - means[1]))
    )
    return (similar, weight)


def smooth_axis(field, axis):
    widths = [(0, 0)] * field.ndim
    widths[axis] = (1, 1)
    padded = jnp.pad(field, widths)
    length = field.shape[axis]
    upper = lax.slice_in_dim(padded, 2, length + 2, axis=axis)
    lower = lax.slice_in_dim(padded, 0, length, axis=axis)
    return 0.25 * lower + 0.5 * field + 0.25 * upper


def regularize(velocity, total, coarse_rows, coarse_cols):
    block_rows = velocity.shape[2] // coarse_rows
    coarse_depth = velocity.shape[1]
    grid = total.reshape(block_rows, GY, 3, coarse_depth, coarse_rows, coarse_cols)
    grid = grid.transpose(2, 3, 0, 4, 1, 5).reshape(velocity.shape)
    regular = smooth_axis(smooth_axis(smooth_axis(grid, 1), 2), 3)
    return velocity + STEP_LENGTH * regular / jnp.sqrt(jnp.mean(regular * regular) + EPSILON)


def per_device(fixed, moving, block_place, tissue):
    slots, planes, row_side, col_side = fixed.shape
    depth_parts = lax.axis_size("gz")
    depth_index = lax.axis_index("gz")
    blocks = slots * lax.axis_size("blk")
    total_planes = planes * depth_parts
    coarse_depth = total_planes // SCALE
    coarse_rows = row_side // SCALE
    coarse_cols = col_side // SCALE
    grid_rows = blocks // GY * coarse_rows
    grid_cols = GY * coarse_cols
    stacked = jnp.stack([fixed, moving], 0)
    reach = 0
    haloed = with_halo(stacked, (("gz", 2),), 5)
    images = haloed.astype(jnp.float32)
    count_w = planes + 2 * (reach + 4)
    count_m = planes + 2 * reach
    fixed_w = images[0, :, 1 : 1 + count_w]
    moving_w = images[1, :, 1 : 1 + count_w]
    depth_slope = 0.5 * (images[1, :, 2 : 2 + count_w] - images[1, :, 0:count_w])
    row_slope = slope(moving_w, 2)
    col_slope = slope(moving_w, 3)
    depth_w = depth_index * planes - (reach + 4) + jnp.arange(count_w)
    inside_w = ((depth_w >= 0) & (depth_w < total_planes)).astype(jnp.float32)
    depth_hat = hat_rows(depth_w.astype(jnp.float32), coarse_depth)
    depth_m = depth_index * planes - reach + jnp.arange(count_m)
    inside_m = ((depth_m >= 0) & (depth_m < total_planes)).astype(jnp.float32)
    row_cells = jnp.arange(row_side)
    col_cells = jnp.arange(col_side)
    block_row = block_place // GY
    block_col = block_place % GY
    row_hat = hat_rows(
        (block_row[:, None] * row_side + row_cells[None, :]).astype(jnp.float32), grid_rows
    )
    col_hat = hat_rows(
        (block_col[:, None] * col_side + col_cells[None, :]).astype(jnp.float32), grid_cols
    )
    own_depth = depth_index * planes + jnp.arange(planes)
    restrict = (own_depth[None, :] // SCALE == jnp.arange(coarse_depth)[:, None]).astype(
        jnp.float32
    )
    box_rows = tap_matrix(row_side, BOX_TAPS)
    box_cols = tap_matrix(col_side, BOX_TAPS)
    gauss_rows = tap_matrix(row_side, GAUSS_TAPS)
    gauss_cols = tap_matrix(col_side, GAUSS_TAPS)
    tissue_scale = tissue.astype(jnp.float32)[:, None, None, None]
    positions = jnp.arange(blocks)
    velocity = jnp.zeros((3, coarse_depth, grid_rows, grid_cols), jnp.float32)
    correlation = jnp.zeros((slots, planes, row_side, col_side), jnp.float32)
    for rounds in range(ITERS):
        partial_value = jnp.einsum("ckab,sxa->sckxb", velocity, row_hat, precision=EXACT)
        partial_value = jnp.einsum("sckxb,syb->sckxy", partial_value, col_hat, precision=EXACT)
        shift = jnp.einsum("zk,sckxy->cszxy", depth_hat, partial_value, precision=EXACT)
        warped = moving_w + shift[0] * depth_slope + shift[1] * row_slope + shift[2] * col_slope
        warped = warped * inside_w[None, :, None, None]
        fields = jnp.stack(
            [fixed_w, warped, fixed_w * fixed_w, warped * warped, fixed_w * warped], 0
        )
        means = planes_filter(fields, BOX_TAPS, count_m)
        means = along_cols(along_rows(means, box_rows), box_cols)
        fixed_m = fixed_w[:, 4 : 4 + count_m]
        warped_m = warped[:, 4 : 4 + count_m]
        similar, weight = statistics(means, fixed_m, warped_m)
        scale = weight * tissue_scale * inside_m[None, :, None, None]
        depth_grad = 0.5 * (warped[:, 5 : 5 + count_m] - warped[:, 3 : 3 + count_m])
        force = jnp.stack(
            [scale * depth_grad, scale * slope(warped_m, 2), scale * slope(warped_m, 3)], 0
        )
        force = with_halo(force, (("gz", 2),), 3)
        smooth = planes_filter(force, GAUSS_TAPS, planes)
        smooth = along_cols(along_rows(smooth, gauss_rows), gauss_cols)
        local = smooth.reshape(3, slots, planes, coarse_rows, SCALE, coarse_cols, SCALE).sum(
            axis=(4, 6)
        )
        piece = jnp.einsum("kp,cspab->sckab", restrict, local, precision=EXACT).reshape(slots, -1)
        onehot_local = (positions[:, None] == block_place[None, :]).astype(jnp.float32)
        local_grid = jnp.dot(onehot_local, piece, precision=EXACT)
        total = lax.psum(local_grid, ("blk", "gz"))
        velocity = regularize(velocity, total, coarse_rows, coarse_cols)
        correlation = similar
    return (velocity, correlation)


def solution(mesh):
    return jax.shard_map(
        per_device,
        mesh=mesh,
        in_specs=(P("blk", "gz", None, None), P("blk", "gz", None, None), P("blk"), P("blk")),
        out_specs=(P(), P("blk", "gz", None, None)),
        check_vma=False,
    )
```

profile of v0, /device:TPU:1, one launch (start us, length us, event | category | flops | bytes accessed | tf_op | source)
XLA Modules:
  0.0 267.4 jit_solution(6952006898740505339)
XLA Ops:
  0.6 0.9 copy_bitcast_fusion
  1.6 4.0 %collective-permute-start = (bf16[2,1,5,32,128]{4,2,3,1,0:T(8,128)(2,1)S(1)}, bf16[2,1,5,32,128]{4,2,3,1,0:T(8,128)(2,1)S(1)}, u32[]{:S(2)}, u32[]{:S(2)}) collective-permute-start(bf16[2,1,5,32,128]{4,2,3,1,0:T(8,128)(2,1)S(1)} %get-tuple-element.38), channel_id=1, source_target_pairs={{0,1},{1,2},{2,3},{4,5},{5,6},{6,7},{8,9},{9,10},{10,11},{12,13},{... | collective-permute-start | bytes 245768 | tf_op jit(solution)/shard_map/ppermute | solution.py:23
  5.7 1.3 collective-permute-start.1
  9.3 0.9 fusion.94
  10.2 1.2 collective-permute-done.1
  13.3 1.0 fusion.6
  14.7 3.5 %collective-permute-start.2 = (f32[3,1,3,32,128]{4,2,3,1,0:T(4,128)S(1)}, f32[3,1,3,32,128]{4,2,3,1,0:T(4,128)S(1)}, u32[]{:S(2)}, u32[]{:S(2)}) collective-permute-start(f32[3,1,3,32,128]{4,2,3,1,0:T(4,128)S(1)} %get-tuple-element.30), channel_id=1, source_target_pairs={{0,1},{1,2},{2,3},{4,5},{5,6},{6,7},{8,9},{9,10},{10,11},{12,13},{... | collective-permute-start | bytes 442376 | tf_op jit(solution)/shard_map/ppermute | solution.py:23
  18.2 1.3 collective-permute-start.3
  19.6 1.3 collective-permute-done.2
  20.8 3.8 %collective-permute-done.3 = f32[3,1,3,32,128]{4,2,3,1,0:T(4,128)S(1)} collective-permute-done((f32[3,1,3,32,128]{4,2,3,1,0:T(4,128)S(1)}, f32[3,1,3,32,128]{4,2,3,1,0:T(4,128)S(1)}, u32[]{:S(2)}, u32[]{:S(2)}) %collective-permute-start.3) | collective-permute-done | bytes 147488 | tf_op jit(solution)/shard_map/ppermute | solution.py:26
  25.6 3.3 %convolution_reduce_fusion.1 = f32[3,8,2,8]{3,2,1,0:T(2,128)S(1)} fusion(f32[3,8,2,16,128,1]{4,3,5,2,1,0:T(8,128)S(1)} %bitcast.237, f32[8,16,128,1,1,1]{2,1,0,5,4,3:T(8,128)S(1)} %bitcast.238), kind=kOutput, calls=%fused_computation.1 | convolution fusion | flops 151092864 | bytes 460288 | tf_op jit(solution)/shard_map/...y,yv->...v/dot_general | solution.py:46
  29.7 1.2 copy.70
  31.0 1.4 reshape.690
  32.3 111.2 %psum.14 = f32[3,2,32,64]{3,2,1,0:T(8,128)S(1)} all-reduce(f32[3,2,32,64]{3,2,1,0:T(8,128)S(1)} %reshape.690), channel_id=1, replica_groups=mesh['blk'=128,'gz'=4] {'blk','gz'}, use_global_device_ids=true, to_apply=%region_1.2 | all-reduce | flops 12288 | bytes 98304 | tf_op jit(solution)/shard_map/psum | solution.py:180
  143.6 0.7 multiply_reduce_fusion.1
  145.8 0.9 convolution_bitcast_fusion
  148.2 1.0 fusion.4
  149.7 1.4 collective-permute-start.4
  151.1 1.3 collective-permute-start.5
  153.1 1.5 collective-permute-done.4
  154.6 3.8 %collective-permute-done.5 = f32[3,1,3,32,128]{4,2,3,1,0:T(4,128)S(1)} collective-permute-done((f32[3,1,3,32,128]{4,2,3,1,0:T(4,128)S(1)}, f32[3,1,3,32,128]{4,2,3,1,0:T(4,128)S(1)}, u32[]{:S(2)}, u32[]{:S(2)}) %collective-permute-start.5) | collective-permute-done | bytes 147488 | tf_op jit(solution)/shard_map/ppermute | solution.py:26
  159.3 3.3 %convolution_reduce_fusion = f32[3,8,2,8]{3,2,1,0:T(2,128)S(1)} fusion(f32[3,8,2,16,128,1]{4,3,5,2,1,0:T(8,128)S(1)} %bitcast.236, f32[8,16,128,1,1,1]{2,1,0,5,4,3:T(8,128)S(1)} %bitcast.239), kind=kOutput, calls=%fused_computation | convolution fusion | flops 151092864 | bytes 460288 | tf_op jit(solution)/shard_map/...y,yv->...v/dot_general | solution.py:46
  164.0 101.1 %psum.15 = f32[3,2,32,64]{3,2,1,0:T(8,128)S(1)} all-reduce(f32[3,2,32,64]{3,2,1,0:T(8,128)S(1)} %reshape.698), channel_id=1, replica_groups=mesh['blk'=128,'gz'=4] {'blk','gz'}, use_global_device_ids=true, to_apply=%region_4.5 | all-reduce | flops 12288 | bytes 98304 | tf_op jit(solution)/shard_map/psum | solution.py:180
  266.6 0.8 divide_add_fusion
  (75 shorter events, 11.2 us)
Async XLA Ops:
  1.6 8.6 %collective-permute-start = (bf16[2,1,5,32,128]{4,2,3,1,0:T(8,128)(2,1)S(1)}, bf16[2,1,5,32,128]{4,2,3,1,0:T(8,128)(2,1)S(1)}, u32[]{:S(2)}, u32[]{:S(2)}) collective-permute-start(bf16[2,1,5,32,128]{4,2,3,1,0:T(8,128)(2,1)S(1)} %get-tuple-element.38), channel_id=1, source_target_pairs={{0,1},{1,2},{2,3},{4,5},{5,6},{6,7},{8,9},{9,10},{10,11},{12,13},{... | collective-permute-start | bytes 245768 | tf_op jit(solution)/shard_map/ppermute | solution.py:23
  5.7 5.7 %collective-permute-start.1 = (bf16[2,1,5,32,128]{4,2,3,1,0:T(8,128)(2,1)S(1)}, bf16[2,1,5,32,128]{4,2,3,1,0:T(8,128)(2,1)S(1)}, u32[]{:S(2)}, u32[]{:S(2)}) collective-permute-start(bf16[2,1,5,32,128]{4,2,3,1,0:T(8,128)(2,1)S(1)} %get-tuple-element.39), channel_id=1, source_target_pairs={{1,0},{2,1},{3,2},{5,4},{6,5},{7,6},{9,8},{10,9},{11,10},{13,12},{... | collective-permute-start | bytes 245768 | tf_op jit(solution)/shard_map/ppermute | solution.py:26
  7.6 2.6 copy-start
  7.8 2.4 copy-start.2
  14.7 6.1 %collective-permute-start.2 = (f32[3,1,3,32,128]{4,2,3,1,0:T(4,128)S(1)}, f32[3,1,3,32,128]{4,2,3,1,0:T(4,128)S(1)}, u32[]{:S(2)}, u32[]{:S(2)}) collective-permute-start(f32[3,1,3,32,128]{4,2,3,1,0:T(4,128)S(1)} %get-tuple-element.30), channel_id=1, source_target_pairs={{0,1},{1,2},{2,3},{4,5},{5,6},{6,7},{8,9},{9,10},{10,11},{12,13},{... | collective-permute-start | bytes 442376 | tf_op jit(solution)/shard_map/ppermute | solution.py:23
  18.2 6.4 %collective-permute-start.3 = (f32[3,1,3,32,128]{4,2,3,1,0:T(4,128)S(1)}, f32[3,1,3,32,128]{4,2,3,1,0:T(4,128)S(1)}, u32[]{:S(2)}, u32[]{:S(2)}) collective-permute-start(f32[3,1,3,32,128]{4,2,3,1,0:T(4,128)S(1)} %get-tuple-element.31), channel_id=1, source_target_pairs={{1,0},{2,1},{3,2},{5,4},{6,5},{7,6},{9,8},{10,9},{11,10},{13,12},{... | collective-permute-start | bytes 442376 | tf_op jit(solution)/shard_map/ppermute | solution.py:26
  29.7 115.3 %copy-start.1 = (f32[32]{0:T(128)S(1)}, f32[32]{0:T(128)}, u32[]{:S(2)}) copy-start(f32[32]{0:T(128)} %copy-done) | copy-start | bytes 388
  29.7 115.3 %copy-start.3 = (f32[32]{0:T(128)S(1)}, f32[32]{0:T(128)}, u32[]{:S(2)}) copy-start(f32[32]{0:T(128)} %copy-done.2) | copy-start | bytes 388
  149.7 4.9 %collective-permute-start.4 = (f32[3,1,3,32,128]{4,2,3,1,0:T(4,128)S(1)}, f32[3,1,3,32,128]{4,2,3,1,0:T(4,128)S(1)}, u32[]{:S(2)}, u32[]{:S(2)}) collective-permute-start(f32[3,1,3,32,128]{4,2,3,1,0:T(4,128)S(1)} %get-tuple-element.26), channel_id=1, source_target_pairs={{0,1},{1,2},{2,3},{4,5},{5,6},{6,7},{8,9},{9,10},{10,11},{12,13},{... | collective-permute-start | bytes 442376 | tf_op jit(solution)/shard_map/ppermute | solution.py:23
  151.1 7.3 %collective-permute-start.5 = (f32[3,1,3,32,128]{4,2,3,1,0:T(4,128)S(1)}, f32[3,1,3,32,128]{4,2,3,1,0:T(4,128)S(1)}, u32[]{:S(2)}, u32[]{:S(2)}) collective-permute-start(f32[3,1,3,32,128]{4,2,3,1,0:T(4,128)S(1)} %get-tuple-element.27), channel_id=1, source_target_pairs={{1,0},{2,1},{3,2},{5,4},{6,5},{7,6},{9,8},{10,9},{11,10},{13,12},{... | collective-permute-start | bytes 442376 | tf_op jit(solution)/shard_map/ppermute | solution.py:26
where the time goes:
time: 268 us; the launch traced here: 267 us
  blocking collectives  212 us (79%)
  matrix products  14.4 us (5%)
  starting transfers between devices  12.8 us (5%)
  waiting for transfers between devices  11.6 us (4%)
  local copies, waits for them, and re-layouts  6.26 us (2%)
  other arithmetic  6.11 us (2%)
  between operations  3.95 us (1%)
    psum x2, blocking collectives, per_device(): total = lax.psum(local_grid, ('blk', 'gz'))  212 us
    ppermute x3, starting transfers between devices, with_halo(): lax.ppermute(lax.slice_in_dim(block, block.shape[dim] - width, None, axis...  8.92 us
    ppermute x3, waiting for transfers between devices, with_halo(): lax.ppermute(lax.slice_in_dim(block, 0, width, axis=dim), axis, backward)  8.79 us
    dot_general x4, matrix products, along_cols(): return jnp.einsum('...y,yv->...v', field, matrix, precision=EXACT)  8.73 us
  transfers between devices with their start and end apart: 6, of which 5 were waited for; matrix products, arithmetic and copies ran while one was open for 1% of the time, Pallas kernels for 0%

commit v1 on v0

--- a/solution.py
+++ b/solution.py
@@ -177,7 +177,9 @@
         piece = jnp.einsum("kp,cspab->sckab", restrict, local, precision=EXACT).reshape(slots, -1)
         onehot_local = (positions[:, None] == block_place[None, :]).astype(jnp.float32)
         local_grid = jnp.dot(onehot_local, piece, precision=EXACT)
-        total = lax.psum(local_grid, ("blk", "gz"))
+        total = local_grid
+        for rr in ("blk", "gz"):
+            total = lax.psum(total, rr)
         velocity = regularize(velocity, total, coarse_rows, coarse_cols)
         correlation = similar
     return (velocity, correlation)

time: 268 us -> 1080 us (4.03)
  blocking collectives: 212 us -> 1020 us
    psum x2 -> x4, blocking collectives: 212 us -> 1020 us  [per_device(): total = lax.psum(total, rr)]
  transfers between devices with their start and end apart: 6 -> 6, of which waited for: 5 -> 5; matrix products, arithmetic and copies ran while one was open for 1% -> 0% of each run, Pallas kernels for 0% -> 0%
where the time goes in v1:
time: 1080 us; the launch traced here: 1070 us
  blocking collectives  1020 us (94%)
  matrix products  14.4 us (1%)
  starting transfers between devices  12.8 us (1%)
    psum x4, blocking collectives, per_device(): total = lax.psum(total, rr)  1020 us
  transfers between devices with their start and end apart: 6, of which 5 were waited for; matrix products, arithmetic and copies ran while one was open for 0% of the time, Pallas kernels for 0%

profile of v1, /device:TPU:1, one launch (start us, length us, event | category | flops | bytes accessed | tf_op | source)
XLA Modules:
  0.0 1072.7 jit_solution(14382476051411386191)
XLA Ops:
  0.6 0.9 copy_bitcast_fusion
  1.6 4.0 collective-permute-start
  5.7 1.3 collective-permute-start.1
  9.3 0.9 fusion.94
  10.2 1.2 collective-permute-done.1
  13.3 1.0 fusion.6
  14.7 3.5 collective-permute-start.2
  18.2 1.3 collective-permute-start.3
  19.6 1.3 collective-permute-done.2
  20.8 3.8 collective-permute-done.3
  25.6 3.3 convolution_reduce_fusion.1
  29.3 496.7 %psum.28 = f32[128,96]{0,1:T(8,128)S(1)} all-reduce(f32[128,96]{0,1:T(8,128)S(1)} %broadcast_multiply_fusion.1), channel_id=1, replica_groups=mesh['blk'=128,'gz'=4] {'blk'}, use_global_device_ids=true, to_apply=%region_1.2 | all-reduce | flops 12288 | bytes 98304 | tf_op jit(solution)/shard_map/psum | solution.py:182
  526.4 1.2 copy.70
  527.7 1.4 reshape.690
  529.0 12.7 %psum.29 = f32[3,2,32,64]{3,2,1,0:T(8,128)S(1)} all-reduce(f32[3,2,32,64]{3,2,1,0:T(8,128)S(1)} %reshape.690), channel_id=1, replica_groups=mesh['blk'=128,'gz'=4] {'gz'}, use_global_device_ids=true, to_apply=%region_2.3 | all-reduce | flops 12288 | bytes 98304 | tf_op jit(solution)/shard_map/psum | solution.py:182
  543.9 0.9 convolution_bitcast_fusion
  546.4 1.0 fusion.4
  547.9 1.4 collective-permute-start.4
  549.3 1.3 collective-permute-start.5
  551.9 3.8 collective-permute-done.5
  556.7 3.3 convolution_reduce_fusion
  560.3 496.1 %psum.30 = f32[128,96]{0,1:T(8,128)S(1)} all-reduce(f32[128,96]{0,1:T(8,128)S(1)} %broadcast_multiply_fusion), channel_id=1, replica_groups=mesh['blk'=128,'gz'=4] {'blk'}, use_global_device_ids=true, to_apply=%region_5.6 | all-reduce | flops 12288 | bytes 98304 | tf_op jit(solution)/shard_map/psum | solution.py:182
  1057.4 13.0 %psum.31 = f32[3,2,32,64]{3,2,1,0:T(8,128)S(1)} all-reduce(f32[3,2,32,64]{3,2,1,0:T(8,128)S(1)} %reshape.698), channel_id=1, replica_groups=mesh['blk'=128,'gz'=4] {'gz'}, use_global_device_ids=true, to_apply=%region_6.7 | all-reduce | flops 12288 | bytes 98304 | tf_op jit(solution)/shard_map/psum | solution.py:182
  1072.0 0.8 divide_add_fusion
  (77 shorter events, 12.6 us)
Async XLA Ops:
  1.6 8.6 collective-permute-start
  5.7 5.7 collective-permute-start.1
  7.6 2.6 copy-start
  7.8 2.4 copy-start.2
  14.7 6.1 collective-permute-start.2
  18.2 6.4 collective-permute-start.3
  526.4 16.8 %copy-start.1 = (f32[32]{0:T(128)S(1)}, f32[32]{0:T(128)}, u32[]{:S(2)}) copy-start(f32[32]{0:T(128)} %copy-done) | copy-start | bytes 388
  526.4 16.8 %copy-start.3 = (f32[32]{0:T(128)S(1)}, f32[32]{0:T(128)}, u32[]{:S(2)}) copy-start(f32[32]{0:T(128)} %copy-done.2) | copy-start | bytes 388
  547.9 4.0 collective-permute-start.4
  549.3 6.4 collective-permute-start.5
